TPU v7x, 256 devices: a whole 4x4x8 slice. The times are simulated.
256 devices in a mesh: dp: 2 (over core), space: 32 (over z, x), feat: 4 (over y).
Axes of the slice: x: 4, y: 4, z: 8, core: 2. Of those that a mesh axis runs over, the one named last changes fastest.
Arguments:
- patches: bfloat16 [4, 192, 360, 1280], P('dp', 'space', 'feat'), parts along dimension 0, may hold values from -6 to 6
- embed_weight: bfloat16 [1280, 1024], replicated
- embed_bias: float32 [1024], replicated
- norm_gain: float32 [1024], replicated, may hold values from 0.1 to 1.9
- norm_bias: float32 [1024], replicated, may hold values from -2 to 2
- w_one: float32 [2, 8, 128, 128], P(None, 'feat'), may hold values from -0.375 to 0.375
- b_one: float32 [2, 8, 128], P(None, 'feat'), may hold values from -3 to 3
- w_two: float32 [2, 8, 128, 128], P(None, 'feat'), may hold values from -0.375 to 0.375
- b_two: float32 [2, 8, 128], P(None, 'feat'), may hold values from -0.6 to 0.6
- lat_cut: int32 [8], P('feat'), may hold values from 32 to 64, as said below
- lon_cut: int32 [8], P('feat'), may hold values from 64 to 128, as said below
Outputs:
- mixed: bfloat16 [4, 192, 360, 1024], P('dp', 'space', None, 'feat'), parts along dimension 0
There are 2 independent parts, one for each index of `dp`. A program takes and returns all parts, laid end to end along the dimension named above; an argument that names none is the same for every part. Nothing has to cross between parts.
Inputs may be any that keep to these rules, and one draw needn't show every extreme that they name: `lat_cut`: some block has bound exactly 64. `lon_cut`: some block has bound exactly 128.
All inputs are finite; a program needn't handle non-finite values.
Results may differ from a plain program's by a relative error of at most 0.0065.
Values may be sent and summed in bfloat16 or wider, within the bound.
A program may use at most 128 MiB of HBM per device.

v0:
```python
import math

import jax
import jax.numpy as jnp
import ml_dtypes
import numpy as np
from jax import lax
from jax.experimental import pallas as pl
from jax.experimental.pallas import tpu as pltpu
from jax.sharding import PartitionSpec as P

MESH = pl.DeviceIdType.MESH
BF = jnp.bfloat16
F32 = jnp.float32

SAMPLES, H, W = 2, 192, 360
PATCH, D = 1280, 1024
KEEP_LAT, KEEP_LON = 64, 128
SHRINK = 0.01
EPSILON = 1e-05

NZ, NX, NY = 8, 4, 4
RS = H // (NZ * NX)
ROWS = SAMPLES * RS
COLS = W // NY
PAD = 96
CH = D // NY
MODES = KEEP_LON // (NZ * NX)
LAG = 5
FWD = 5
STEP = 2


def split(table):
    high = table.astype(ml_dtypes.bfloat16)
    low = (table - high.astype(np.float64)).astype(ml_dtypes.bfloat16)
    return high, low


def phase_tables():
    lon = np.full((NY, PAD), 0)
    for q in range(NY):
        lon[q, :COLS] = q * COLS + np.arange(COLS)
    real_col = np.broadcast_to(np.arange(PAD) < COLS, (NY, PAD)).reshape(-1)
    lon = lon.reshape(-1)
    g = np.arange(KEEP_LON)
    ang = 2.0 * math.pi * ((g[:, None] * lon[None, :]) % W) / W
    fwd = np.stack([np.cos(ang), -np.sin(ang)], axis=1) * real_col / math.sqrt(W)
    fwd = fwd.reshape(2 * KEEP_LON, NY * PAD)
    gx = np.arange(KEEP_LON).reshape(NZ, NX, MODES).transpose(1, 0, 2).reshape(-1)
    ang = 2.0 * math.pi * ((lon[:, None] * gx[None, :]) % W) / W
    weight = np.where(gx == 0, 1.0, 2.0) / math.sqrt(W)
    inv = np.stack([np.cos(ang) * weight, -np.sin(ang) * weight], axis=2) * real_col[:, None, None]
    inv = inv.reshape(NY * PAD, 2 * KEEP_LON)
    lat = np.arange(H).reshape(NZ, NX, RS).transpose(1, 2, 0).reshape(-1)
    f = np.concatenate([np.arange(KEEP_LAT), np.arange(-KEEP_LAT, 0)])
    ang = 2.0 * math.pi * ((f[:, None] * lat[None, :]) % H) / H
    c, s = np.cos(ang) / math.sqrt(H), np.sin(ang) / math.sqrt(H)
    lat_fwd = np.concatenate([np.concatenate([c, s], 1), np.concatenate([-s, c], 1)], 0)
    c, s = c.T, s.T
    lat_inv = np.concatenate([np.concatenate([c, -s], 1), np.concatenate([s, c], 1)], 0)
    wide = np.stack([*split(fwd), *split(lat_fwd)])
    tall = np.stack([*split(lat_inv), *split(inv)])
    return wide, tall


def dot(a, b):
    return jnp.dot(a, b, preferred_element_type=F32)


def halves(value):
    high = value.astype(BF)
    return high, (value - high.astype(F32)).astype(BF)


def complex_weight(w_ref, k):
    re, im = w_ref[0, k], w_ref[1, k]
    return jnp.concatenate(
        [jnp.concatenate([re, im], axis=1), jnp.concatenate([-im, re], axis=1)], axis=0
    )


def kernel(
    p_hbm, w_hbm, eb_ref, gain_ref, shift_ref, w1_ref, b1_ref, w2_ref, b2_ref, latc, lonc, wide_hbm, tall_hbm,
    out_hbm,
    pbuf, wbuf, wide, tall, zs, zr, st, sb, zr1, xr1, rel, xs2, xr2, fr, ob, flat, w1h, w1l, w2h, w2l,
    pat_sem, wgt_sem, tab_sem, send_sem, y_sem, st_sem, z1_sem, x1_sem, x2_sem, z2_sem, out_sem,
):
    space = lax.axis_index("space")
    yi = lax.axis_index("feat")
    zi, xi = space // NX, lax.rem(space, NX)
    y_peer = lambda d: lax.rem(yi + d, NY)
    z_peer = lambda d: lax.rem(zi + d, NZ)
    x_peer = lambda d: lax.rem(xi + d, NX)
    y_id = lambda y: {"feat": y}
    z_id = lambda z: {"space": z * NX + xi}
    x_id = lambda x: {"space": zi * NX + x}
    Y_ORDER, X_ORDER, Z_ORDER = (2, 1, 3), (2, 1, 3), (4, 3, 5, 2, 6, 1, 7)

    def remote(src, dst, sends, recv, where):
        pltpu.make_async_remote_copy(
            src_ref=src, dst_ref=dst, send_sem=send_sem.at[sends], recv_sem=recv, device_id=where, device_id_type=MESH
        ).start()

    def patch_copy(r):
        return pltpu.make_async_copy(p_hbm.at[r], pbuf.at[r], pat_sem.at[r])

    patch_copy(0).start()
    weight_copy = pltpu.make_async_copy(w_hbm, wbuf, wgt_sem)
    weight_copy.start()

    barrier = pltpu.get_barrier_semaphore()
    for d in Y_ORDER:
        pl.semaphore_signal(barrier, inc=1, device_id=y_id(y_peer(d)), device_id_type=MESH)
    for d in Z_ORDER:
        pl.semaphore_signal(barrier, inc=1, device_id=z_id(z_peer(d)), device_id_type=MESH)
    for d in X_ORDER:
        pl.semaphore_signal(barrier, inc=1, device_id=x_id(x_peer(d)), device_id_type=MESH)

    @pl.loop(1, ROWS)
    def _(r):
        patch_copy(r).start()

    wide_copy = pltpu.make_async_copy(wide_hbm, wide, tab_sem.at[0])
    tall_copy = pltpu.make_async_copy(tall_hbm, tall, tab_sem.at[1])
    wide_copy.start()
    tall_copy.start()

    @pl.loop(0, ROWS)
    def _(r):
        for q in range(NY):
            zs[r, q, 80:, :] = jnp.zeros((PAD - 80, CH), BF)
        zr[r, yi, 80:, :] = jnp.zeros((PAD - 80, CH), BF)

    for k in range(2):
        w1h[k], w1l[k] = halves(complex_weight(w1_ref, k))
        w2h[k], w2l[k] = halves(complex_weight(w2_ref, k))
    st[yi] = jnp.zeros((PAD, 128), F32)
    lane = lax.broadcasted_iota(jnp.int32, (PAD, 128), 1)
    channels = pl.ds(pl.multiple_of(yi * CH, CH), CH)

    pl.semaphore_wait(barrier, len(Y_ORDER) + len(Z_ORDER) + len(X_ORDER))
    weight_copy.wait()

    def embed(r):
        patch_copy(r).wait()
        e = dot(pbuf[r], wbuf[...]) + eb_ref[...]
        mean = jnp.mean(e, axis=1, keepdims=True)
        e = e - mean
        var = jnp.mean(e * e, axis=1, keepdims=True) + EPSILON
        inv = lax.rsqrt(var)
        z = (e * inv).astype(BF)
        for q in range(NY):
            zs[r, q, 0:COLS, :] = z[:, q * CH : (q + 1) * CH]
        for d in Y_ORDER:
            remote(zs.at[r, y_peer(d)], zr.at[r, yi], 0, y_sem.at[r], y_id(y_peer(d)))
        zr[r, yi] = zs[r, yi]
        part = lane[0:COLS]
        old = st[yi, 0:COLS]
        st[yi, 0:COLS] = jnp.where(part == 2 * r, var * inv, jnp.where(part == 2 * r + 1, mean, old))

    def to_modes(r):
        pltpu.make_async_copy(zr.at[r, 0 : NY - 1], zr.at[r, 0 : NY - 1], y_sem.at[r]).wait()
        z = zr[r].reshape(NY * PAD, CH).astype(F32)
        n = (z * gain_ref[:, channels] + shift_ref[:, channels]).astype(BF)
        s = (dot(wide[0], n) + dot(wide[1], n)).reshape(NZ * NX, 2 * MODES, CH)
        s = jnp.concatenate([s[:, :, 0:128], s[:, :, 128:256]], axis=1).astype(BF)
        sb[r] = s.reshape(NZ, NX, 16, 128)
        for d in Z_ORDER:
            remote(sb.at[r, z_peer(d)], zr1.at[:, r, zi], 1, z1_sem.at[r], z_id(z_peer(d)))
        pltpu.make_async_copy(sb.at[r, zi], zr1.at[:, r, zi], z1_sem.at[r]).start()

    def pass_on(r):
        pltpu.make_async_copy(zr1.at[:, r], zr1.at[:, r], z1_sem.at[r]).wait()
        for d in X_ORDER:
            remote(zr1.at[x_peer(d), r], xr1.at[xi, r], 2, x1_sem.at[r], x_id(x_peer(d)))
        pltpu.make_async_copy(zr1.at[xi, r], xr1.at[xi, r], x1_sem.at[r]).start()

    def mix(s):
        rows = pl.ds(s * RS, RS)
        for i in range(RS):
            r = s * RS + i
            pltpu.make_async_copy(xr1.at[:, r], xr1.at[:, r], x1_sem.at[r]).wait()
        n = RS * NZ * 16
        for x in range(NX):
            rel[x * n : (x + 1) * n, :] = xr1[x, rows].astype(F32).reshape(n, 128)
        outs = []
        for k in range(2):
            cols = []
            for m in range(MODES):
                both = [rel[pl.ds(k * 8 + m * 2 + i, H, stride=16), :].astype(BF) for i in range(2)]
                cols.append(jnp.concatenate(both, axis=0))
            data = jnp.concatenate(cols, axis=1)
            g = dot(wide[2], data) + dot(wide[3], data)
            v = jnp.concatenate(
                [
                    jnp.concatenate([g[0:128, m * 128 : (m + 1) * 128], g[128:256, m * 128 : (m + 1) * 128]], axis=1)
                    for m in range(MODES)
                ],
                axis=0,
            )
            for first, (wh, wl, b_ref) in enumerate(((w1h, w1l, b1_ref), (w2h, w2l, b2_ref))):
                vh, vl = halves(v)
                bias = jnp.concatenate([b_ref[0, k : k + 1], b_ref[1, k : k + 1]], axis=1)
                v = dot(vh, wh[k]) + dot(vl, wh[k]) + dot(vh, wl[k]) + bias
                if first == 0:
                    v = jnp.maximum(v, 0.0)
            v = v - jnp.clip(v, -SHRINK, SHRINK)
            f = lax.broadcasted_iota(jnp.int32, (128, 1), 0)
            f = jnp.where(f < KEEP_LAT, f, 2 * KEEP_LAT - f)
            keep_lat = f < latc[k]
            cols = []
            for m in range(MODES):
                part = v[m * 128 : (m + 1) * 128]
                keep = jnp.logical_and(keep_lat, space * MODES + m < lonc[k])
                part = jnp.where(keep, part, 0.0)
                cols.append(jnp.concatenate([part[:, 0:128], part[:, 128:256]], axis=0))
            oh, ol = halves(jnp.concatenate(cols, axis=1))
            outs.append(dot(tall[0], oh) + dot(tall[1], oh) + dot(tall[0], ol))
        for k in range(2):
            for m in range(MODES):
                for i in range(2):
                    rel[pl.ds(k * 8 + m * 2 + i, H, stride=16), :] = outs[k][
                        i * H : (i + 1) * H, m * 128 : (m + 1) * 128
                    ]
        for x in range(NX):
            xs2[x, rows] = rel[x * n : (x + 1) * n, :].reshape(RS, NZ, 16, 128).astype(BF)
        for j in range(RS // STEP):
            some = pl.ds(s * RS + j * STEP, STEP)
            sem = x2_sem.at[s * (RS // STEP) + j]
            for d in X_ORDER:
                remote(xs2.at[x_peer(d), some], xr2.at[xi, some], 3, sem, x_id(x_peer(d)))
            pltpu.make_async_copy(xs2.at[xi, some], xr2.at[xi, some], sem).start()

    def send_back(j):
        some = pl.ds(j * STEP, STEP)
        pltpu.make_async_copy(xr2.at[:, some], xr2.at[:, some], x2_sem.at[j]).wait()
        for d in Z_ORDER:
            remote(xr2.at[:, some, z_peer(d)], fr.at[:, some, zi], 4, z2_sem.at[j], z_id(z_peer(d)))
        pltpu.make_async_copy(xr2.at[:, some, zi], fr.at[:, some, zi], z2_sem.at[j]).start()

    def out_copy(r):
        return pltpu.make_async_copy(ob.at[r], out_hbm.at[r], out_sem)

    def to_tokens(r):
        a = fr[:, r].astype(F32).reshape(NX * NZ, 16, 128)
        a = jnp.concatenate([a[:, 0:8], a[:, 8:16]], axis=2).reshape(2 * KEEP_LON, CH).astype(BF)
        filtered = dot(tall[2], a) + dot(tall[3], a)
        for q in range(NY):
            stat = st[q]
            std = jnp.sum(jnp.where(lane == 2 * r, stat, 0.0), axis=1, keepdims=True)
            mean = jnp.sum(jnp.where(lane == 2 * r + 1, stat, 0.0), axis=1, keepdims=True)
            mixed = filtered[q * PAD : (q + 1) * PAD] + (zr[r, q].astype(F32) * std + mean)
            flat[q * COLS : (q + 1) * COLS, :] = mixed[0:COLS]
        ob[r] = flat[...].astype(BF)
        out_copy(r).start()

    def finish(j):
        some = pl.ds(j * STEP, STEP)
        pltpu.make_async_copy(fr.at[:, some], fr.at[:, some], z2_sem.at[j]).wait()

        @pl.loop(0, STEP)
        def _(i):
            to_tokens(j * STEP + i)

    @pl.loop(0, ROWS + LAG)
    def _(i):
        @pl.when(i < ROWS)
        def _():
            embed(i)

        @pl.when(i == ROWS - 1)
        def _():
            for d in Y_ORDER:
                remote(st.at[yi], st.at[yi], 5, st_sem, y_id(y_peer(d)))

        @pl.when(i == LAG)
        def _():
            wide_copy.wait()

        @pl.when(i >= LAG)
        def _():
            to_modes(i - LAG)

        @pl.when(i >= LAG + FWD)
        def _():
            pass_on(i - LAG - FWD)

    tall_copy.wait()
    half = RS // STEP
    mix(0)

    @pl.loop(ROWS - FWD, ROWS)
    def _(r):
        pass_on(r)

    @pl.loop(0, half)
    def _(j):
        send_back(j)

    mix(1)
    pltpu.make_async_copy(st.at[0 : NY - 1], st.at[0 : NY - 1], st_sem).wait()
    finish(0)

    @pl.loop(half, 2 * half)
    def _(j):
        send_back(j)

    @pl.loop(1, 2 * half)
    def _(j):
        finish(j)

    for sends, ref in enumerate(
        (
            zs.at[:, 0 : NY - 1],
            sb.at[:, 0 : NZ - 1],
            zr1.at[0 : NX - 1],
            xs2.at[0 : NX - 1],
            xr2.at[:, :, 0 : NZ - 1],
            st.at[0 : NY - 1],
        )
    ):
        pltpu.make_async_copy(ref, ref, send_sem.at[sends]).wait()
    pltpu.make_async_copy(ob, out_hbm, out_sem).wait()


def solution(mesh):
    wide, tall = phase_tables()

    def local(
        patches, embed_weight, embed_bias, norm_gain, norm_bias, w_one, b_one, w_two, b_two, lat_cut, lon_cut
    ):
        anywhere = pl.BlockSpec(memory_space=pl.ANY)
        vmem = pl.BlockSpec(memory_space=pltpu.VMEM)
        smem = pl.BlockSpec(memory_space=pltpu.SMEM)
        back = (NX, ROWS, NZ, 16, 128)
        out = pl.pallas_call(
            kernel,
            out_shape=jax.ShapeDtypeStruct((ROWS, W, CH), BF),
            in_specs=[anywhere, anywhere] + [vmem] * 7 + [smem, smem, anywhere, anywhere],
            out_specs=anywhere,
            scratch_shapes=[
                pltpu.VMEM((ROWS, COLS, PATCH), BF),
                pltpu.VMEM((PATCH, D), BF),
                pltpu.VMEM((4, 256, 384), BF),
                pltpu.VMEM((4, 384, 256), BF),
                pltpu.VMEM((ROWS, NY, PAD, CH), BF),
                pltpu.VMEM((ROWS, NY, PAD, CH), BF),
                pltpu.VMEM((NY, PAD, 128), F32),
                pltpu.VMEM((ROWS, NZ, NX, 16, 128), BF),
                pltpu.VMEM(back, BF),
                pltpu.VMEM(back, BF),
                pltpu.VMEM((H * 16, 128), F32),
                pltpu.VMEM(back, BF),
                pltpu.VMEM(back, BF),
                pltpu.VMEM(back, BF),
                pltpu.VMEM((ROWS, W, CH), BF),
                pltpu.VMEM((W, CH), F32),
            ]
            + [pltpu.VMEM((2, 256, 256), BF)] * 4
            + [
                pltpu.SemaphoreType.DMA((ROWS,)),
                pltpu.SemaphoreType.DMA,
                pltpu.SemaphoreType.DMA((2,)),
                pltpu.SemaphoreType.DMA((6,)),
                pltpu.SemaphoreType.DMA((ROWS,)),
                pltpu.SemaphoreType.DMA,
                pltpu.SemaphoreType.DMA((ROWS,)),
                pltpu.SemaphoreType.DMA((ROWS,)),
                pltpu.SemaphoreType.DMA((ROWS // STEP,)),
                pltpu.SemaphoreType.DMA((ROWS // STEP,)),
                pltpu.SemaphoreType.DMA,
            ],
            compiler_params=pltpu.CompilerParams(
                collective_id=0, has_side_effects=True, vmem_limit_bytes=56 * 1024 * 1024
            ),
            name="afno",
        )(
            patches.reshape(ROWS, COLS, PATCH),
            embed_weight,
            embed_bias.reshape(1, D),
            norm_gain.reshape(1, D),
            norm_bias.reshape(1, D),
            w_one,
            b_one,
            w_two,
            b_two,
            lat_cut,
            lon_cut,
            jnp.asarray(wide),
            jnp.asarray(tall),
        )
        return out.reshape(SAMPLES, RS, W, CH)

    in_specs = (
        P("dp", "space", "feat", None),
        P(),
        P(),
        P(),
        P(),
        P(None, "feat", None, None),
        P(None, "feat", None),
        P(None, "feat", None, None),
        P(None, "feat", None),
        P("feat"),
        P("feat"),
    )
    return jax.shard_map(
        local, mesh=mesh, in_specs=in_specs, out_specs=P("dp", "space", None, "feat"), check_vma=False
    )
```

profile of v0, /device:TPU:6, one launch (start us, length us, event | category | flops | bytes accessed | tf_op | source)
XLA Modules:
  0.0 94.3 jit_solution(17665745872211333451)
XLA Ops:
  0.0 3.8 %copy.14 = bf16[2,6,90,1280]{3,2,1,0:T(8,128)(2,1)} copy(bf16[2,6,90,1280]{3,0,2,1:T(2,128)(2,1)} %param.13) | data formatting | bytes 5529600 | tf_op args[0]
  3.8 87.4 %afno.1 = bf16[12,360,256]{2,1,0:T(8,128)(2,1)} custom-call(bf16[12,90,1280]{2,1,0:T(8,128)(2,1)} %bitcast.5, bf16[1280,1024]{1,0:T(8,128)(2,1)} %w_hbm.1, f32[1,1024]{1,0:T(1,128)} %bitcast.7, f32[1,1024]{1,0:T(1,128)} %bitcast.8, f32[1,1024]{1,0:T(1,128)} %bitcast.9, f32[2,2,128,128]{3,2,1,0:T(8,128)} %w1_ref.1, f32[2,2,128]{2,1,0:T(2,128)} %b1_ref.1, ...), custom_call_target="tpu_custom_call" | custom-call | tf_op jit(solution)/shard_map/afno/pallas_call | solution.py:337
  91.2 3.1 %copy.16 = bf16[2,6,360,256]{3,2,1,0:T(8,128)(2,1)} copy(bf16[2,6,360,256]{3,2,1,0:T(8,128)(2,1)} %bitcast.6) | data formatting | bytes 4423680
where the time goes:
time: 94.5 us; the launch traced here: 94.3 us
  Pallas kernels  87.4 us (92%)
  local copies, waits for them, and re-layouts  6.93 us (7%)
    pallas_call x1, Pallas kernels, local(): pl.pallas_call(kernel, out_shape=jax.ShapeDtypeStruct((ROWS, W, CH), BF),...  87.4 us
    unnamed x2, local copies, waits for them, and re-layouts  6.93 us

commit v1 on v0

--- a/solution.py
+++ b/solution.py
@@ -26,7 +26,9 @@
 PAD = 96
 CH = D // NY
 MODES = KEEP_LON // (NZ * NX)
-LAG = 5
+LANES = 128
+PARTS = PATCH // LANES
+LAG = 3
 FWD = 5
 STEP = 2
 
@@ -81,9 +83,10 @@
 
 
 def kernel(
-    p_hbm, w_hbm, eb_ref, gain_ref, shift_ref, w1_ref, b1_ref, w2_ref, b2_ref, latc, lonc, wide_hbm, tall_hbm,
+    p_hbm, w_hbm, eb_ref, gain_ref, shift_ref, w1_hbm, b1_ref, w2_hbm, b2_ref, latc, lonc, wide_hbm, tall_hbm,
     out_hbm,
-    pbuf, wbuf, wide, tall, zs, zr, st, sb, zr1, xr1, rel, xs2, xr2, fr, ob, flat, w1h, w1l, w2h, w2l,
+    pbuf, xb, ez, wbuf, w1_ref, w2_ref, wide, tall, zs, zr, st, sb, zr1, xr1, rel, xs2, xr2, fr, ob, flat,
+    w1h, w1l, w2h, w2l,
     pat_sem, wgt_sem, tab_sem, send_sem, y_sem, st_sem, z1_sem, x1_sem, x2_sem, z2_sem, out_sem,
 ):
     space = lax.axis_index("space")
@@ -102,10 +105,11 @@
             src_ref=src, dst_ref=dst, send_sem=send_sem.at[sends], recv_sem=recv, device_id=where, device_id_type=MESH
         ).start()
 
-    def patch_copy(r):
-        return pltpu.make_async_copy(p_hbm.at[r], pbuf.at[r], pat_sem.at[r])
-
-    patch_copy(0).start()
+    def patch_copies(r):
+        for c in range(PARTS):
+            pltpu.make_async_copy(p_hbm.at[r, :, c], pbuf.at[r, c], pat_sem.at[r]).start()
+
+    patch_copies(0)
     weight_copy = pltpu.make_async_copy(w_hbm, wbuf, wgt_sem)
     weight_copy.start()
 
@@ -117,14 +121,18 @@
     for d in X_ORDER:
         pl.semaphore_signal(barrier, inc=1, device_id=x_id(x_peer(d)), device_id_type=MESH)
 
-    @pl.loop(1, ROWS)
+    @pl.loop(1, RS)
     def _(r):
-        patch_copy(r).start()
+        patch_copies(r)
 
     wide_copy = pltpu.make_async_copy(wide_hbm, wide, tab_sem.at[0])
     tall_copy = pltpu.make_async_copy(tall_hbm, tall, tab_sem.at[1])
+    w1_copy = pltpu.make_async_copy(w1_hbm, w1_ref, tab_sem.at[2])
+    w2_copy = pltpu.make_async_copy(w2_hbm, w2_ref, tab_sem.at[3])
     wide_copy.start()
     tall_copy.start()
+    w1_copy.start()
+    w2_copy.start()
 
     @pl.loop(0, ROWS)
     def _(r):
@@ -132,32 +140,45 @@
             zs[r, q, 80:, :] = jnp.zeros((PAD - 80, CH), BF)
         zr[r, yi, 80:, :] = jnp.zeros((PAD - 80, CH), BF)
 
-    for k in range(2):
-        w1h[k], w1l[k] = halves(complex_weight(w1_ref, k))
-        w2h[k], w2l[k] = halves(complex_weight(w2_ref, k))
     st[yi] = jnp.zeros((PAD, 128), F32)
     lane = lax.broadcasted_iota(jnp.int32, (PAD, 128), 1)
     channels = pl.ds(pl.multiple_of(yi * CH, CH), CH)
 
-    pl.semaphore_wait(barrier, len(Y_ORDER) + len(Z_ORDER) + len(X_ORDER))
     weight_copy.wait()
 
     def embed(r):
-        patch_copy(r).wait()
-        e = dot(pbuf[r], wbuf[...]) + eb_ref[...]
+        pltpu.make_async_copy(pbuf.at[r], pbuf.at[r], pat_sem.at[r]).wait()
+        for c in range(PARTS):
+            xb[:, c * LANES : (c + 1) * LANES] = pbuf[r, c].reshape(2 * COLS, LANES)
+        e = dot(xb[...], wbuf[...]) + eb_ref[...]
         mean = jnp.mean(e, axis=1, keepdims=True)
         e = e - mean
         var = jnp.mean(e * e, axis=1, keepdims=True) + EPSILON
         inv = lax.rsqrt(var)
-        z = (e * inv).astype(BF)
-        for q in range(NY):
-            zs[r, q, 0:COLS, :] = z[:, q * CH : (q + 1) * CH]
+        z = e * inv
+        for c in range(D // LANES):
+            ez[c] = z[:, c * LANES : (c + 1) * LANES]
+        at = lax.broadcasted_iota(jnp.int32, (2 * COLS, LANES), 1)
+        ez[D // LANES] = jnp.where(at == 0, var * inv, mean)
+        for s in range(SAMPLES):
+            row = s * RS + r
+            for c in range(D // LANES):
+                q, half = c // 2, c % 2
+                zs[row, q, 0:COLS, half * LANES : (half + 1) * LANES] = ez[c, pl.ds(s, COLS, stride=2), :].astype(BF)
+            zr[row, yi] = zs[row, yi]
+            stat = ez[D // LANES, pl.ds(s, COLS, stride=2), :]
+            std, mean_s = stat[:, 0:1], stat[:, 1:2]
+            part = lane[0:COLS]
+            old = st[yi, 0:COLS]
+            st[yi, 0:COLS] = jnp.where(part == 2 * row, std, jnp.where(part == 2 * row + 1, mean_s, old))
+
+    def send_tokens(r):
         for d in Y_ORDER:
             remote(zs.at[r, y_peer(d)], zr.at[r, yi], 0, y_sem.at[r], y_id(y_peer(d)))
-        zr[r, yi] = zs[r, yi]
-        part = lane[0:COLS]
-        old = st[yi, 0:COLS]
-        st[yi, 0:COLS] = jnp.where(part == 2 * r, var * inv, jnp.where(part == 2 * r + 1, mean, old))
+
+    embed(0)
+    wide_copy.wait()
+    pl.semaphore_wait(barrier, len(Y_ORDER) + len(Z_ORDER) + len(X_ORDER))
 
     def to_modes(r):
         pltpu.make_async_copy(zr.at[r, 0 : NY - 1], zr.at[r, 0 : NY - 1], y_sem.at[r]).wait()
@@ -267,16 +288,24 @@
     def _(i):
         @pl.when(i < ROWS)
         def _():
-            embed(i)
+            send_tokens(i)
+
+        @pl.when(i < RS - 1)
+        def _():
+            embed(i + 1)
+
+        @pl.when(i == RS)
+        def _():
+            w1_copy.wait()
+            w2_copy.wait()
+            for k in range(2):
+                w1h[k], w1l[k] = halves(complex_weight(w1_ref, k))
+                w2h[k], w2l[k] = halves(complex_weight(w2_ref, k))
 
         @pl.when(i == ROWS - 1)
         def _():
             for d in Y_ORDER:
                 remote(st.at[yi], st.at[yi], 5, st_sem, y_id(y_peer(d)))
-
-        @pl.when(i == LAG)
-        def _():
-            wide_copy.wait()
 
         @pl.when(i >= LAG)
         def _():
@@ -330,18 +359,22 @@
     def local(
         patches, embed_weight, embed_bias, norm_gain, norm_bias, w_one, b_one, w_two, b_two, lat_cut, lon_cut
     ):
-        anywhere = pl.BlockSpec(memory_space=pl.ANY)
+        anywhere = pl.BlockSpec(memory_space=pltpu.HBM)
         vmem = pl.BlockSpec(memory_space=pltpu.VMEM)
         smem = pl.BlockSpec(memory_space=pltpu.SMEM)
         back = (NX, ROWS, NZ, 16, 128)
         out = pl.pallas_call(
             kernel,
             out_shape=jax.ShapeDtypeStruct((ROWS, W, CH), BF),
-            in_specs=[anywhere, anywhere] + [vmem] * 7 + [smem, smem, anywhere, anywhere],
-            out_specs=anywhere,
+            in_specs=[anywhere, anywhere, vmem, vmem, vmem, anywhere, vmem, anywhere, vmem, smem, smem, anywhere, anywhere],
+            out_specs=pl.BlockSpec(memory_space=pl.ANY),
             scratch_shapes=[
-                pltpu.VMEM((ROWS, COLS, PATCH), BF),
+                pltpu.VMEM((RS, PARTS, COLS, SAMPLES, LANES), BF),
+                pltpu.VMEM((2 * COLS, PATCH), BF),
+                pltpu.VMEM((D // LANES + 1, 2 * COLS, LANES), F32),
                 pltpu.VMEM((PATCH, D), BF),
+                pltpu.VMEM((2, 2, 128, 128), F32),
+                pltpu.VMEM((2, 2, 128, 128), F32),
                 pltpu.VMEM((4, 256, 384), BF),
                 pltpu.VMEM((4, 384, 256), BF),
                 pltpu.VMEM((ROWS, NY, PAD, CH), BF),
@@ -359,9 +392,9 @@
             ]
             + [pltpu.VMEM((2, 256, 256), BF)] * 4
             + [
-                pltpu.SemaphoreType.DMA((ROWS,)),
+                pltpu.SemaphoreType.DMA((RS,)),
                 pltpu.SemaphoreType.DMA,
-                pltpu.SemaphoreType.DMA((2,)),
+                pltpu.SemaphoreType.DMA((4,)),
                 pltpu.SemaphoreType.DMA((6,)),
                 pltpu.SemaphoreType.DMA((ROWS,)),
                 pltpu.SemaphoreType.DMA,
@@ -372,11 +405,11 @@
                 pltpu.SemaphoreType.DMA,
             ],
             compiler_params=pltpu.CompilerParams(
-                collective_id=0, has_side_effects=True, vmem_limit_bytes=56 * 1024 * 1024
+                collective_id=0, has_side_effects=True, vmem_limit_bytes=54 * 1024 * 1024
             ),
             name="afno",
         )(
-            patches.reshape(ROWS, COLS, PATCH),
+            patches.reshape(SAMPLES, RS, COLS, PARTS, LANES).transpose(1, 2, 3, 0, 4),
             embed_weight,
             embed_bias.reshape(1, D),
             norm_gain.reshape(1, D),

time: 94.5 us -> 90.7 us (0.960)
  local copies, waits for them, and re-layouts: 6.93 us -> 3.12 us
    unnamed x2 -> x1, local copies, waits for them, and re-layouts: 6.93 us -> 3.12 us
where the time goes in v1:
time: 90.7 us; the launch traced here: 90.3 us
  Pallas kernels  87.1 us (96%)
  local copies, waits for them, and re-layouts  3.12 us (3%)
    pallas_call x1, Pallas kernels, local(): pl.pallas_call(kernel, out_shape=jax.ShapeDtypeStruct((ROWS, W, CH), BF),...  87.1 us
    unnamed x1, local copies, waits for them, and re-layouts  3.12 us

profile of v1, /device:TPU:6, one launch (start us, length us, event | category | flops | bytes accessed | tf_op | source)
XLA Modules:
  0.0 90.3 jit_solution(13055385892603170018)
XLA Ops:
  0.0 87.1 %afno.1 = bf16[12,360,256]{2,1,0:T(8,128)(2,1)} custom-call(bf16[6,90,10,2,128]{4,3,2,1,0:T(2,128)(2,1)} %bitcast.8, bf16[1280,1024]{1,0:T(8,128)(2,1)} %w_hbm.1, f32[1,1024]{1,0:T(1,128)} %bitcast.9, f32[1,1024]{1,0:T(1,128)} %bitcast.10, f32[1,1024]{1,0:T(1,128)} %bitcast.11, f32[2,2,128,128]{3,2,1,0:T(8,128)} %w1_hbm.1, f32[2,2,128]{2,1,0:T(2,128)} %b1_ref.1, ...), custom_call_target="tpu_custom_call" | custom-call | tf_op jit(solution)/shard_map/afno/pallas_call | solution.py:366
  87.2 3.1 %copy.15 = bf16[2,6,360,256]{3,2,1,0:T(8,128)(2,1)} copy(bf16[2,6,360,256]{3,2,1,0:T(8,128)(2,1)} %bitcast.7) | data formatting | bytes 4423680

commit v2 on v1

--- a/solution.py
+++ b/solution.py
@@ -1,3 +1,4 @@
+import functools
 import math
 
 import jax
@@ -28,9 +29,10 @@
 MODES = KEEP_LON // (NZ * NX)
 LANES = 128
 PARTS = PATCH // LANES
-LAG = 3
-FWD = 5
-STEP = 2
+LAG = 2
+FWD = 4
+OUT_GROUPS = ((0, 1), (1, 2), (2, 4), (4, 6), (6, 8), (8, 10), (10, 11), (11, 12))
+BACK_GROUPS = ((0, 1), (1, 3), (3, 6), (6, 7), (7, 9), (9, 11), (11, 12))
 
 
 def split(table):
@@ -186,22 +188,32 @@
         n = (z * gain_ref[:, channels] + shift_ref[:, channels]).astype(BF)
         s = (dot(wide[0], n) + dot(wide[1], n)).reshape(NZ * NX, 2 * MODES, CH)
         s = jnp.concatenate([s[:, :, 0:128], s[:, :, 128:256]], axis=1).astype(BF)
-        sb[r] = s.reshape(NZ, NX, 16, 128)
+        s = s.reshape(NZ, NX, 16, 128)
+        for x in range(NX):
+            sb[x, r] = s[:, x]
+
+    def some_rows(groups, g):
+        return pl.ds(groups[g][0], groups[g][1] - groups[g][0])
+
+    def send_modes(g):
+        rows = some_rows(OUT_GROUPS, g)
         for d in Z_ORDER:
-            remote(sb.at[r, z_peer(d)], zr1.at[:, r, zi], 1, z1_sem.at[r], z_id(z_peer(d)))
-        pltpu.make_async_copy(sb.at[r, zi], zr1.at[:, r, zi], z1_sem.at[r]).start()
-
-    def pass_on(r):
-        pltpu.make_async_copy(zr1.at[:, r], zr1.at[:, r], z1_sem.at[r]).wait()
+            remote(sb.at[:, rows, z_peer(d)], zr1.at[:, rows, zi], 1, z1_sem.at[g], z_id(z_peer(d)))
+        pltpu.make_async_copy(sb.at[:, rows, zi], zr1.at[:, rows, zi], z1_sem.at[g]).start()
+
+    def pass_on(g):
+        rows = some_rows(OUT_GROUPS, g)
+        pltpu.make_async_copy(zr1.at[:, rows], zr1.at[:, rows], z1_sem.at[g]).wait()
         for d in X_ORDER:
-            remote(zr1.at[x_peer(d), r], xr1.at[xi, r], 2, x1_sem.at[r], x_id(x_peer(d)))
-        pltpu.make_async_copy(zr1.at[xi, r], xr1.at[xi, r], x1_sem.at[r]).start()
+            remote(zr1.at[x_peer(d), rows], xr1.at[xi, rows], 2, x1_sem.at[g], x_id(x_peer(d)))
+        pltpu.make_async_copy(zr1.at[xi, rows], xr1.at[xi, rows], x1_sem.at[g]).start()
 
     def mix(s):
         rows = pl.ds(s * RS, RS)
-        for i in range(RS):
-            r = s * RS + i
-            pltpu.make_async_copy(xr1.at[:, r], xr1.at[:, r], x1_sem.at[r]).wait()
+        for g, (low, _) in enumerate(OUT_GROUPS):
+            if low // RS == s:
+                some = some_rows(OUT_GROUPS, g)
+                pltpu.make_async_copy(xr1.at[:, some], xr1.at[:, some], x1_sem.at[g]).wait()
         n = RS * NZ * 16
         for x in range(NX):
             rel[x * n : (x + 1) * n, :] = xr1[x, rows].astype(F32).reshape(n, 128)
@@ -246,15 +258,15 @@
                     ]
         for x in range(NX):
             xs2[x, rows] = rel[x * n : (x + 1) * n, :].reshape(RS, NZ, 16, 128).astype(BF)
-        for j in range(RS // STEP):
-            some = pl.ds(s * RS + j * STEP, STEP)
-            sem = x2_sem.at[s * (RS // STEP) + j]
-            for d in X_ORDER:
-                remote(xs2.at[x_peer(d), some], xr2.at[xi, some], 3, sem, x_id(x_peer(d)))
-            pltpu.make_async_copy(xs2.at[xi, some], xr2.at[xi, some], sem).start()
+        for j, (low, _) in enumerate(BACK_GROUPS):
+            if low // RS == s:
+                some = some_rows(BACK_GROUPS, j)
+                for d in X_ORDER:
+                    remote(xs2.at[x_peer(d), some], xr2.at[xi, some], 3, x2_sem.at[j], x_id(x_peer(d)))
+                pltpu.make_async_copy(xs2.at[xi, some], xr2.at[xi, some], x2_sem.at[j]).start()
 
     def send_back(j):
-        some = pl.ds(j * STEP, STEP)
+        some = some_rows(BACK_GROUPS, j)
         pltpu.make_async_copy(xr2.at[:, some], xr2.at[:, some], x2_sem.at[j]).wait()
         for d in Z_ORDER:
             remote(xr2.at[:, some, z_peer(d)], fr.at[:, some, zi], 4, z2_sem.at[j], z_id(z_peer(d)))
@@ -276,14 +288,6 @@
         ob[r] = flat[...].astype(BF)
         out_copy(r).start()
 
-    def finish(j):
-        some = pl.ds(j * STEP, STEP)
-        pltpu.make_async_copy(fr.at[:, some], fr.at[:, some], z2_sem.at[j]).wait()
-
-        @pl.loop(0, STEP)
-        def _(i):
-            to_tokens(j * STEP + i)
-
     @pl.loop(0, ROWS + LAG)
     def _(i):
         @pl.when(i < ROWS)
@@ -311,38 +315,40 @@
         def _():
             to_modes(i - LAG)
 
-        @pl.when(i >= LAG + FWD)
-        def _():
-            pass_on(i - LAG - FWD)
+        for g, (_, high) in enumerate(OUT_GROUPS):
+            pl.when(i == LAG + high - 1)(functools.partial(send_modes, g))
+            if high + FWD <= ROWS:
+                pl.when(i == LAG + high - 1 + FWD)(functools.partial(pass_on, g))
 
     tall_copy.wait()
-    half = RS // STEP
     mix(0)
-
-    @pl.loop(ROWS - FWD, ROWS)
+    pass_on(5)
+    send_back(0)
+    send_back(1)
+    pass_on(6)
+    send_back(2)
+    pass_on(7)
+    mix(1)
+    send_back(3)
+    pltpu.make_async_copy(st.at[0 : NY - 1], st.at[0 : NY - 1], st_sem).wait()
+
+    @pl.loop(0, ROWS)
     def _(r):
-        pass_on(r)
-
-    @pl.loop(0, half)
-    def _(j):
-        send_back(j)
-
-    mix(1)
-    pltpu.make_async_copy(st.at[0 : NY - 1], st.at[0 : NY - 1], st_sem).wait()
-    finish(0)
-
-    @pl.loop(half, 2 * half)
-    def _(j):
-        send_back(j)
-
-    @pl.loop(1, 2 * half)
-    def _(j):
-        finish(j)
+        for j, (low, _) in enumerate(BACK_GROUPS):
+
+            @pl.when(r == low)
+            def _(j=j):
+                some = some_rows(BACK_GROUPS, j)
+                pltpu.make_async_copy(fr.at[:, some], fr.at[:, some], z2_sem.at[j]).wait()
+
+        to_tokens(r)
+        for j in range(4, len(BACK_GROUPS)):
+            pl.when(r == j - 4)(functools.partial(send_back, j))
 
     for sends, ref in enumerate(
         (
             zs.at[:, 0 : NY - 1],
-            sb.at[:, 0 : NZ - 1],
+            sb.at[:, :, 0 : NZ - 1],
             zr1.at[0 : NX - 1],
             xs2.at[0 : NX - 1],
             xr2.at[:, :, 0 : NZ - 1],
@@ -351,6 +357,16 @@
     ):
         pltpu.make_async_copy(ref, ref, send_sem.at[sends]).wait()
     pltpu.make_async_copy(ob, out_hbm, out_sem).wait()
+
+
+def copy_rows(src, dst, held, in_sem, out_sem):
+    for r in range(ROWS):
+        pltpu.make_async_copy(src.at[r], held.at[r], in_sem.at[r]).start()
+    for r in range(ROWS):
+        pltpu.make_async_copy(src.at[r], held.at[r], in_sem.at[r]).wait()
+        pltpu.make_async_copy(held.at[r], dst.at[r], out_sem.at[r]).start()
+    for r in range(ROWS):
+        pltpu.make_async_copy(held.at[r], dst.at[r], out_sem.at[r]).wait()
 
 
 def solution(mesh):
@@ -380,7 +396,7 @@
                 pltpu.VMEM((ROWS, NY, PAD, CH), BF),
                 pltpu.VMEM((ROWS, NY, PAD, CH), BF),
                 pltpu.VMEM((NY, PAD, 128), F32),
-                pltpu.VMEM((ROWS, NZ, NX, 16, 128), BF),
+                pltpu.VMEM(back, BF),
                 pltpu.VMEM(back, BF),
                 pltpu.VMEM(back, BF),
                 pltpu.VMEM((H * 16, 128), F32),
@@ -398,10 +414,10 @@
                 pltpu.SemaphoreType.DMA((6,)),
                 pltpu.SemaphoreType.DMA((ROWS,)),
                 pltpu.SemaphoreType.DMA,
-                pltpu.SemaphoreType.DMA((ROWS,)),
-                pltpu.SemaphoreType.DMA((ROWS,)),
-                pltpu.SemaphoreType.DMA((ROWS // STEP,)),
-                pltpu.SemaphoreType.DMA((ROWS // STEP,)),
+                pltpu.SemaphoreType.DMA((len(OUT_GROUPS),)),
+                pltpu.SemaphoreType.DMA((len(OUT_GROUPS),)),
+                pltpu.SemaphoreType.DMA((len(BACK_GROUPS),)),
+                pltpu.SemaphoreType.DMA((len(BACK_GROUPS),)),
                 pltpu.SemaphoreType.DMA,
             ],
             compiler_params=pltpu.CompilerParams(
@@ -423,6 +439,18 @@
             jnp.asarray(wide),
             jnp.asarray(tall),
         )
+        out = pl.pallas_call(
+            copy_rows,
+            out_shape=jax.ShapeDtypeStruct((ROWS, W, CH), BF),
+            in_specs=[anywhere],
+            out_specs=pl.BlockSpec(memory_space=pl.ANY),
+            scratch_shapes=[
+                pltpu.VMEM((ROWS, W, CH), BF),
+                pltpu.SemaphoreType.DMA((ROWS,)),
+                pltpu.SemaphoreType.DMA((ROWS,)),
+            ],
+            name="copy_rows",
+        )(out)
         return out.reshape(SAMPLES, RS, W, CH)
 
     in_specs = (

time: 90.7 us -> 89.1 us (0.982)
  local copies, waits for them, and re-layouts: 3.12 us -> 0 us
  Pallas kernels: 87.1 us -> 88.8 us
    unnamed x1 -> x0, local copies, waits for them, and re-layouts: 3.12 us -> none
    pallas_call x0 -> x1, Pallas kernels: none -> 2.57 us  [local(): pl.pallas_call(copy_rows, out_shape=jax.ShapeDtypeStruct((ROWS, W, CH), B...]
    pallas_call x1, Pallas kernels: 87.1 us -> 86.2 us  [local(): pl.pallas_call(kernel, out_shape=jax.ShapeDtypeStruct((ROWS, W, CH), BF),...]
where the time goes in v2:
time: 89.1 us; the launch traced here: 88.8 us
  Pallas kernels  88.8 us (100%)
    pallas_call x1, Pallas kernels, local(): pl.pallas_call(kernel, out_shape=jax.ShapeDtypeStruct((ROWS, W, CH), BF),...  86.2 us
    pallas_call x1, Pallas kernels, local(): pl.pallas_call(copy_rows, out_shape=jax.ShapeDtypeStruct((ROWS, W, CH), B...  2.57 us

profile of v2, /device:TPU:6, one launch (start us, length us, event | category | flops | bytes accessed | tf_op | source)
XLA Modules:
  0.0 88.8 jit_solution(16033310377012554387)
XLA Ops:
  0.0 86.2 %afno.1.src = bf16[12,360,256]{2,1,0:T(8,128)(2,1)} custom-call(bf16[6,90,10,2,128]{4,3,2,1,0:T(2,128)(2,1)} %bitcast.7, bf16[1280,1024]{1,0:T(8,128)(2,1)} %w_hbm.1, f32[1,1024]{1,0:T(1,128)} %bitcast.8, f32[1,1024]{1,0:T(1,128)} %bitcast.9, f32[1,1024]{1,0:T(1,128)} %bitcast.10, f32[2,2,128,128]{3,2,1,0:T(8,128)} %w1_hbm.1, f32[2,2,128]{2,1,0:T(2,128)} %b1_ref.1, ...), custom_call_target="tpu_custom_call" | custom-call | tf_op jit(solution)/shard_map/afno/pallas_call | solution.py:382
  86.2 2.6 %copy_rows.1 = bf16[12,360,256]{2,1,0:T(8,128)(2,1)} custom-call(bf16[12,360,256]{2,1,0:T(8,128)(2,1)} %afno.1.src), custom_call_target="tpu_custom_call" | custom-call | tf_op jit(solution)/shard_map/copy_rows/pallas_call | solution.py:442

commit v3 on v2

--- a/solution.py
+++ b/solution.py
@@ -32,6 +32,7 @@
 LAG = 2
 FWD = 4
 OUT_GROUPS = ((0, 1), (1, 2), (2, 4), (4, 6), (6, 8), (8, 10), (10, 11), (11, 12))
+COPY = 3
 BACK_GROUPS = ((0, 1), (1, 3), (3, 6), (6, 7), (7, 9), (9, 11), (11, 12))
 
 
@@ -248,8 +249,8 @@
                 keep = jnp.logical_and(keep_lat, space * MODES + m < lonc[k])
                 part = jnp.where(keep, part, 0.0)
                 cols.append(jnp.concatenate([part[:, 0:128], part[:, 128:256]], axis=0))
-            oh, ol = halves(jnp.concatenate(cols, axis=1))
-            outs.append(dot(tall[0], oh) + dot(tall[1], oh) + dot(tall[0], ol))
+            oh = jnp.concatenate(cols, axis=1).astype(BF)
+            outs.append(dot(tall[0], oh) + dot(tall[1], oh))
         for k in range(2):
             for m in range(MODES):
                 for i in range(2):
@@ -360,13 +361,14 @@
 
 
 def copy_rows(src, dst, held, in_sem, out_sem):
-    for r in range(ROWS):
-        pltpu.make_async_copy(src.at[r], held.at[r], in_sem.at[r]).start()
-    for r in range(ROWS):
-        pltpu.make_async_copy(src.at[r], held.at[r], in_sem.at[r]).wait()
-        pltpu.make_async_copy(held.at[r], dst.at[r], out_sem.at[r]).start()
-    for r in range(ROWS):
-        pltpu.make_async_copy(held.at[r], dst.at[r], out_sem.at[r]).wait()
+    pieces = [pl.ds(i * COPY, COPY) for i in range(ROWS // COPY)]
+    for i, rows in enumerate(pieces):
+        pltpu.make_async_copy(src.at[rows], held.at[rows], in_sem.at[i]).start()
+    for i, rows in enumerate(pieces):
+        pltpu.make_async_copy(src.at[rows], held.at[rows], in_sem.at[i]).wait()
+        pltpu.make_async_copy(held.at[rows], dst.at[rows], out_sem.at[i]).start()
+    for i, rows in enumerate(pieces):
+        pltpu.make_async_copy(held.at[rows], dst.at[rows], out_sem.at[i]).wait()
 
 
 def solution(mesh):

time: 89.1 us -> 89.1 us (level)
  no operation moved by 1% of the time
where the time goes in v3:
time: 89.1 us; the launch traced here: 88.9 us
  Pallas kernels  88.9 us (100%)
    pallas_call x1, Pallas kernels, local(): pl.pallas_call(kernel, out_shape=jax.ShapeDtypeStruct((ROWS, W, CH), BF),...  86.3 us
    pallas_call x1, Pallas kernels, local(): pl.pallas_call(copy_rows, out_shape=jax.ShapeDtypeStruct((ROWS, W, CH), B...  2.61 us

profile of v3, /device:TPU:6, one launch (start us, length us, event | category | flops | bytes accessed | tf_op | source)
XLA Modules:
  0.0 88.9 jit_solution(11404452946960506954)
XLA Ops:
  0.0 86.3 %afno.1.src = bf16[12,360,256]{2,1,0:T(8,128)(2,1)} custom-call(bf16[6,90,10,2,128]{4,3,2,1,0:T(2,128)(2,1)} %bitcast.7, bf16[1280,1024]{1,0:T(8,128)(2,1)} %w_hbm.1, f32[1,1024]{1,0:T(1,128)} %bitcast.8, f32[1,1024]{1,0:T(1,128)} %bitcast.9, f32[1,1024]{1,0:T(1,128)} %bitcast.10, f32[2,2,128,128]{3,2,1,0:T(8,128)} %w1_hbm.1, f32[2,2,128]{2,1,0:T(2,128)} %b1_ref.1, ...), custom_call_target="tpu_custom_call" | custom-call | tf_op jit(solution)/shard_map/afno/pallas_call | solution.py:384
  86.3 2.6 %copy_rows.1 = bf16[12,360,256]{2,1,0:T(8,128)(2,1)} custom-call(bf16[12,360,256]{2,1,0:T(8,128)(2,1)} %afno.1.src), custom_call_target="tpu_custom_call" | custom-call | tf_op jit(solution)/shard_map/copy_rows/pallas_call | solution.py:444
